TPU v7x, 256 devices: a whole 4x4x8 slice. The times are simulated.
256 devices in a mesh: dp: 16 (over x, y_lo, core), mp: 16 (over z, y_hi).
Axes of the slice: x: 4, y: 4 (y_hi: 2, y_lo: 2; y = y_hi * 2 + y_lo), z: 8, core: 2. Of those that a mesh axis runs over, the one named last changes fastest.
Arguments:
- block_input: bfloat16 [4096, 6144], P('dp'), may hold values from -6 to 6
- qkv_weight: bfloat16 [3, 6144, 4096], P(None, None, 'mp'), may hold values from -0.078125 to 0.078125
- grad_attn: bfloat16 [4096, 4096], P('dp', 'mp'), may hold values from -6 to 6
Outputs:
- grad_input: bfloat16 [4096, 6144], P('dp')
- grad_qkv: bfloat16 [3, 6144, 4096], P(None, 'dp', 'mp')
All inputs are finite; a program needn't handle non-finite values.
Results may differ from a plain program's by a relative error of at most 0.025.
Values may be sent and summed in bfloat16 or wider, within the bound.
A program may use at most 128 MiB of HBM per device.

v0:
```python
import math

import jax
import jax.numpy as jnp
from jax import lax
from jax.sharding import PartitionSpec as P

HD = 128
PATCH = 256


EPSILON = 1e-06


def normalize(values):
    row_mean = jnp.mean(values, axis=-1, keepdims=True)
    centered = values - row_mean
    inv_std = lax.rsqrt(jnp.mean(centered * centered, axis=-1, keepdims=True) + EPSILON)
    return (centered * inv_std, inv_std)


def norm_back(upstream, normed, inv_std):
    mean_grad = jnp.mean(upstream, axis=-1, keepdims=True)
    mean_cross = jnp.mean(upstream * normed, axis=-1, keepdims=True)
    return inv_std * (upstream - mean_grad - normed * mean_cross)


def head_grads(normed_rows, qkv_weight, grad_attn):
    num_rows = normed_rows.shape[0]
    inner_width = qkv_weight.shape[2]
    frames = num_rows // PATCH
    num_heads = inner_width // HD
    factor = 1.0 / math.sqrt(HD)
    projected = jnp.einsum(
        "td,cde->cte", normed_rows, qkv_weight, preferred_element_type=jnp.float32
    ).astype(jnp.bfloat16)
    shaped = projected.reshape(3, frames, PATCH, num_heads, HD)
    q_hat, q_inv = normalize(shaped[0].astype(jnp.float32))
    k_hat, k_inv = normalize(shaped[1].astype(jnp.float32))
    q_low = q_hat.astype(jnp.bfloat16)
    k_low = k_hat.astype(jnp.bfloat16)
    scores = (
        jnp.einsum("fqhd,fkhd->fhqk", q_low, k_low, preferred_element_type=jnp.float32) * factor
    )
    exp_scores = jnp.exp(scores)
    attn_probs = exp_scores / jnp.sum(exp_scores, axis=-1, keepdims=True)
    probs_low = attn_probs.astype(jnp.bfloat16)
    grad_out = grad_attn.reshape(frames, PATCH, num_heads, HD)
    grad_probs = jnp.einsum(
        "fqhd,fkhd->fhqk", grad_out, shaped[2], preferred_element_type=jnp.float32
    )
    grad_v = jnp.einsum("fhqk,fqhd->fkhd", probs_low, grad_out, preferred_element_type=jnp.float32)
    row_term = jnp.sum(attn_probs * grad_probs, axis=-1, keepdims=True)
    grad_scores = (attn_probs * (grad_probs - row_term) * factor).astype(jnp.bfloat16)
    grad_qhat = jnp.einsum(
        "fhqk,fkhd->fqhd", grad_scores, k_low, preferred_element_type=jnp.float32
    )
    grad_khat = jnp.einsum(
        "fhqk,fqhd->fkhd", grad_scores, q_low, preferred_element_type=jnp.float32
    )
    grad_q = norm_back(grad_qhat, q_hat, q_inv)
    grad_k = norm_back(grad_khat, k_hat, k_inv)
    stacked = jnp.stack([grad_q, grad_k, grad_v], axis=2)
    return stacked.reshape(num_rows, 3, inner_width).astype(jnp.bfloat16)


def on_device(block_input, qkv_weight, grad_attn):
    x_hat, x_inv = normalize(block_input.astype(jnp.float32))
    normed = x_hat.astype(jnp.bfloat16)
    grad_proj = head_grads(normed, qkv_weight, grad_attn)
    input_terms = jnp.einsum(
        "tce,cde->td", grad_proj, qkv_weight, preferred_element_type=jnp.float32
    )
    grad_normed = lax.psum(input_terms.astype(jnp.bfloat16), "mp").astype(jnp.float32)
    grad_input = norm_back(grad_normed, x_hat, x_inv).astype(jnp.bfloat16)
    partial_grad = jnp.einsum("td,tce->cde", normed, grad_proj, preferred_element_type=jnp.float32)
    grad_qkv = lax.psum_scatter(
        partial_grad.astype(jnp.bfloat16), "dp", scatter_dimension=1, tiled=True
    )
    return (grad_input, grad_qkv)


def solution(mesh):
    placed = (P("dp", None), P(None, None, "mp"), P("dp", "mp"))
    return jax.shard_map(
        on_device,
        mesh=mesh,
        in_specs=placed,
        out_specs=(P("dp", None), P(None, "dp", "mp")),
        check_vma=False,
    )
```

profile of v0, /device:TPU:14, one launch (start us, length us, event | category | flops | bytes accessed | tf_op | source)
XLA Modules:
  0.0 344.1 jit_solution(2799974412335876231)
XLA Ops:
  8.0 0.0 copy-start
  8.0 0.0 all-reduce.2.cloned.1.call-start
  8.1 2.5 convert_reduce_fusion.1
  10.6 2.9 fusion.10
  13.5 0.0 copy-done
  13.5 0.0 copy-start.4
  13.5 0.0 copy-start.3
  13.5 7.7 %fusion.24 = bf16[3,256,256]{1,2,0:T(8,128)(2,1)S(1)} fusion(bf16[3,6144,256]{2,1,0:T(8,128)(2,1)} %param.4, bf16[256,6144]{1,0:T(8,128)(2,1)S(1)} %copy-done, f32[256]{0:T(256)S(1)} %add_rsqrt_fusion.2, f32[256]{0:T(256)S(1)} %broadcast_multiply_fusion.8), kind=kOutput, calls=%fused_computation.29 | convolution fusion | flops 2422407168 | bytes 12978176 | tf_op jit(solution)/shard_map/td,cde->cte/dot_general | solution.py:34
  21.2 0.0 copy-done.4
  21.2 0.0 copy-start.2
  21.2 0.7 copy-done.2
  22.0 0.8 fusion.46
  22.8 1.0 reduce_sum.130
  23.7 1.0 multiply_reduce_fusion.3
  24.8 0.6 reduce_sum.128
  25.4 0.7 broadcast_multiply_fusion.5
  26.1 0.6 add_rsqrt_fusion.1
  26.7 0.0 copy-done.3
  26.7 0.8 copy.44
  27.5 1.6 multiply_convert_fusion.2
  29.1 2.0 fusion.33
  31.1 2.0 convolution_bitcast_fusion.1
  33.2 3.3 fusion.45
  36.5 3.3 fusion.44
  39.7 2.0 fusion.19
  41.7 0.7 broadcast_multiply_fusion
  42.4 0.7 broadcast_multiply_fusion.1
  43.0 0.7 broadcast_multiply_fusion.2
  43.7 0.7 broadcast_multiply_fusion.3
  44.4 1.3 multiply_convert_fusion.1
  45.7 0.1 copy.28
  45.8 0.1 copy.29
  45.9 2.2 convolution_convert_fusion.1
  48.1 1.0 copy.30
  49.1 0.0 copy-start.5
  49.1 11.1 %fusion.2 = bf16[256,6144]{1,0:T(8,128)(2,1)} fusion(bf16[3,6144,256]{2,1,0:T(8,128)(2,1)} %param.4, bf16[256,1,256]{2,0,1:T(8,128)(2,1)S(1)} %copy.30, bf16[256,1,256]{2,0,1:T(8,128)(2,1)S(1)} %copy.29, bf16[256,1,256]{2,0,1:T(8,128)(2,1)S(1)} %copy.28), kind=kOutput, calls=%fused_computation.9 | convolution fusion | flops 2417885184 | bytes 12976128 | tf_op jit(solution)/shard_map/tce,cde->td/dot_general | solution.py:71
  60.2 0.0 all-reduce.2.cloned.1.call-update
  60.2 0.2 reduce-scatter.4.cloned.1.call-start
  60.4 0.0 copy-done.5
  60.4 5.3 %fusion.1 = bf16[3,6144,256]{1,2,0:T(8,128)(2,1)} fusion(bf16[256,6144]{1,0:T(8,128)(2,1)S(1)} %copy-done, f32[256]{0:T(256)S(1)} %copy-done.5, f32[256]{0:T(256)S(1)} %broadcast_multiply_fusion.8, bf16[256,1,256]{2,0,1:T(8,128)(2,1)S(1)} %copy.30, bf16[256,1,256]{2,0,1:T(8,128)(2,1)S(1)} %copy.29, bf16[256,1,256]{2,0,1:T(8,128)(2,1)S(1)} %copy.28), kind=kOutput, calls=%fused_computation.5 | convolution fusion | flops 2427322368 | bytes 12978176 | tf_op jit(solution)/shard_map/td,tce->cde/dot_general | solution.py:76
  65.7 19.1 %copy.41 = bf16[3,6144,256]{2,0,1:T(4,128)(2,1)} copy(bf16[3,6144,256]{1,2,0:T(8,128)(2,1)} %fusion.1) | data formatting | bytes 18874368
  84.8 11.0 %copy.45 = bf16[768,8,3,256]{3,1,2,0:T(8,128)(2,1)} copy(bf16[768,8,3,256]{3,2,1,0:T(4,128)(2,1)} %bitcast.60) | data formatting | bytes 18874368
  95.9 0.0 reduce-scatter.4.cloned.1.call-update
  95.9 231.0 %all-reduce.2.cloned.1.call-done = bf16[256,6144]{1,0:T(8,128)(2,1)} async-done(((bf16[256,6144]{1,0:T(8,128)(2,1)}), bf16[256,6144]{1,0:T(8,128)(2,1)}) %all-reduce.2.cloned.1.call-update) | async-done | bytes 3145744 | tf_op jit(solution)/shard_map/psum | solution.py:74
  326.9 0.0 copy-start.1
  326.9 4.0 %convert_reduce_fusion = (f32[256]{0:T(256)S(1)}, f32[256]{0:T(256)S(1)}) fusion(bf16[256,6144]{1,0:T(8,128)(2,1)} %all-reduce.2.cloned.1.call-done, f32[256]{0:T(256)S(1)} %copy-done.5, f32[256]{0:T(256)S(1)} %broadcast_multiply_fusion.8, bf16[256,6144]{1,0:T(8,128)(2,1)S(1)} %copy-done), kind=kLoop, calls=%fused_computation.4 | loop fusion | flops 11009536 | bytes 6295552 | tf_op jit(solution)/shard_map/reduce_sum | solution.py:23
  330.9 0.0 copy-done.1
  330.9 3.6 %fusion.9 = bf16[256,6144]{1,0:T(8,128)(2,1)} fusion(bf16[256,6144]{1,0:T(8,128)(2,1)S(1)} %copy-done, bf16[256,6144]{1,0:T(8,128)(2,1)S(1)} %copy-done.1, f32[256]{0:T(256)S(1)} %broadcast_multiply_fusion.6, f32[256]{0:T(256)S(1)} %broadcast_multiply_fusion.7, f32[256]{0:T(256)S(1)} %copy-done.5, f32[256]{0:T(256)S(1)} %broadcast_multiply_fusion.8), kind=kLoop, calls=%fused_computation.16 | loop fusion | flops 14155776 | bytes 9441280 | tf_op jit(solution)/shard_map/convert_element_type | solution.py:75
  334.5 0.0 reduce-scatter.4.cloned.1.call-done
  334.5 1.2 reshape.278
  335.8 0.9 copy.32
  (7 shorter events, 0.1 us)
Async XLA Ops:
  8.0 5.5 %copy-start = (bf16[256,6144]{1,0:T(8,128)(2,1)S(1)}, bf16[256,6144]{1,0:T(8,128)(2,1)}, u32[]{:S(2)}) copy-start(bf16[256,6144]{1,0:T(8,128)(2,1)} %param.3) | copy-start | bytes 9437188
  8.0 318.9 %all-reduce.2.cloned.1.call-start = ((), (), s32[]{:S(2)}) async-start(), calls=%async_computation.1 | async-start | bytes 6291456 | tf_op jit(solution)/shard_map/psum | solution.py:74
  13.5 7.7 %copy-start.4 = (f32[256]{0:T(256)}, f32[256]{0:T(256)S(1)}, u32[]{:S(2)}) copy-start(f32[256]{0:T(256)S(1)} %add_rsqrt_fusion.2) | copy-start | bytes 3076
  13.5 13.2 %copy-start.3 = (bf16[256,256]{1,0:T(8,128)(2,1)S(1)}, bf16[256,256]{1,0:T(8,128)(2,1)}, u32[]{:S(2)}) copy-start(bf16[256,256]{1,0:T(8,128)(2,1)} %param.5) | copy-start | bytes 393220
  21.2 0.7 copy-start.2
  49.1 11.4 %copy-start.5 = (f32[256]{0:T(256)S(1)}, f32[256]{0:T(256)}, u32[]{:S(2)}) copy-start(f32[256]{0:T(256)} %copy-done.4) | copy-start | bytes 3076
  60.2 274.3 %reduce-scatter.4.cloned.1.call-start = ((), (), s32[]{:S(2)}) async-start(), calls=%async_computation.2 | async-start | bytes 10027008
  326.9 4.1 %copy-start.1 = (bf16[256,6144]{1,0:T(8,128)(2,1)S(1)}, bf16[256,6144]{1,0:T(8,128)(2,1)}, u32[]{:S(2)}) copy-start(bf16[256,6144]{1,0:T(8,128)(2,1)} %all-reduce.2.cloned.1.call-done) | copy-start | bytes 9437188
Sparse Core Ops, SparseCore 0:
  60.3 266.5 all-reduce.1
Sparse Core Ops, SparseCore 1:
  96.0 173.9 reduce-scatter.3
where the time goes:
time: 345 us; the launch traced here: 344 us
  waiting for transfers between devices  231 us (67%)
  matrix products  38.9 us (11%)
  local copies, waits for them, and re-layouts  35 us (10%)
  other arithmetic  23.4 us (7%)
  between operations  15.6 us (5%)
    psum x1, waiting for transfers between devices, on_device(): lax.psum(input_terms.astype(jnp.bfloat16), 'mp').astype(jnp.float32)  231 us
    unnamed x16, local copies, waits for them, and re-layouts  33 us
    dot_general x1, matrix products, on_device(): jnp.einsum('tce,cde->td', grad_proj, qkv_weight, preferred_element_type=j...  11.1 us
    dot_general x1, matrix products, head_grads(): jnp.einsum('td,cde->cte', normed_rows, qkv_weight, preferred_element_type...  7.7 us
  transfers between devices with their start and end apart: 2, of which 1 were waited for; matrix products, arithmetic and copies ran while one was open for 13% of the time, Pallas kernels for 0%

commit v1 on v0

v1 whole, which is shorter than its diff:
```python
import functools
import math

import jax
import jax.numpy as jnp
from jax import lax
from jax.experimental import pallas as pl
from jax.experimental.pallas import tpu as pltpu
from jax.sharding import PartitionSpec as P

MESH = pl.DeviceIdType.MESH
F32 = jnp.float32
BF16 = jnp.bfloat16
EPSILON = 1e-06

NX, NZ = 4, 8
ROWS = 256
D = 6144
HALF = D // 2
INNER = 256
HD = 128
OWN = 16
SLICE = 384
EH = 384


def normalize(values):
    row_mean = jnp.mean(values, axis=-1, keepdims=True)
    centered = values - row_mean
    inv_std = lax.rsqrt(jnp.mean(centered * centered, axis=-1, keepdims=True) + EPSILON)
    return centered * inv_std, inv_std


def norm_back(upstream, normed, inv_std):
    mean_grad = jnp.mean(upstream, axis=-1, keepdims=True)
    mean_cross = jnp.mean(upstream * normed, axis=-1, keepdims=True)
    return inv_std * (upstream - mean_grad - normed * mean_cross)


def dot(a, b, ca, cb):
    return lax.dot_general(a, b, (((ca,), (cb,)), ((), ())), preferred_element_type=F32)


def head_grads(q, k, v, g):
    factor = 1.0 / math.sqrt(HD)
    q_hat, q_inv = normalize(q.astype(F32))
    k_hat, k_inv = normalize(k.astype(F32))
    q_low = q_hat.astype(BF16)
    k_low = k_hat.astype(BF16)
    exp_scores = jnp.exp(dot(q_low, k_low, 1, 1) * factor)
    probs = exp_scores / jnp.sum(exp_scores, axis=-1, keepdims=True)
    grad_probs = dot(g, v, 1, 1)
    grad_v = dot(probs.astype(BF16), g, 0, 0)
    row_term = jnp.sum(probs * grad_probs, axis=-1, keepdims=True)
    grad_scores = (probs * (grad_probs - row_term) * factor).astype(BF16)
    grad_q = norm_back(dot(grad_scores, k_low, 1, 0), q_hat, q_inv)
    grad_k = norm_back(dot(grad_scores, q_low, 0, 0), k_hat, k_inv)
    return grad_q, grad_k, grad_v


def kernel(
    x_hbm, w_hbm, g_hbm, gi_hbm, gw_hbm,
    xv, wv, gv, nv, pv, gp, gp2, nr, tv, slots, ry, og, bp, rb, yb, xh, xinv, gwv,
    x_sem, w_sem, g_sem, o_sem, q_sem,
    core_s, core_r, rs_s, rs_r, ry_s, ry_r, ag_s, ag_r, ay_s, ay_r, b_s, b_r, by_s, by_r,
):
    dp, mp = lax.axis_index("dp"), lax.axis_index("mp")
    x, yl, c = dp // 4, (dp // 2) % 2, dp % 2
    z, yh = mp // 2, mp % 2

    def at(x_, yl_, c_, z_, yh_):
        return ((x_ * 2 + yl_) * 2 + c_, z_ * 2 + yh_)

    to_z = (at(x, yl, c, (z + 1) % NZ, yh), at(x, yl, c, (z + NZ - 1) % NZ, yh))
    to_x = (at((x + 1) % NX, yl, c, z, yh), at((x + NX - 1) % NX, yl, c, z, yh))
    to_yh = at(x, yl, c, z, 1 - yh)
    to_yl = at(x, 1 - yl, c, z, yh)
    to_core = at(x, yl, 1 - c, z, yh)

    x_copies = []
    for i in range(4):
        rows = pl.ds(i * 64, 64)
        x_copies.append(pltpu.make_async_copy(x_hbm.at[rows], xv.at[rows], x_sem.at[i]))
    w_copies = [pltpu.make_async_copy(w_hbm.at[i], wv.at[i], w_sem.at[i]) for i in range(3)]
    g_copy = pltpu.make_async_copy(g_hbm, gv, g_sem)
    for cp in x_copies + w_copies + [g_copy]:
        cp.start()

    barrier = pltpu.get_barrier_semaphore()
    neighbours = to_z + to_x + (to_yh, to_yl, to_core)
    for d in neighbours:
        pl.semaphore_signal(barrier, inc=1, device_id=d, device_id_type=MESH)

    sends = []

    def remote(src, dst, s, r, d):
        cp = pltpu.make_async_remote_copy(
            src_ref=src, dst_ref=dst, send_sem=s, recv_sem=r, device_id=d, device_id_type=MESH
        )
        cp.start()
        sends.append(cp)
        return cp

    for i in range(4):
        x_copies[i].wait()
        rows = pl.ds(i * 64, 64)
        nv[rows, :] = normalize(xv[rows, :].astype(F32))[0].astype(BF16)

    pl.semaphore_wait(barrier, len(neighbours))
    core = []
    for i in range(8):
        cols = pl.ds(pl.multiple_of((i * 2 + 1 - c) * SLICE, 128), SLICE)
        core.append(
            remote(nv.at[:, cols], nr.at[:, pl.ds(i * SLICE, SLICE)], core_s.at[i], core_r.at[i], to_core)
        )

    for i in range(3):
        w_copies[i].wait()
        pv[:, pl.ds(i * INNER, INNER)] = dot(nv[...], wv[i], 1, 0).astype(BF16)
    g_copy.wait()
    for h in range(2):
        cols = [pl.ds(i * INNER + h * HD, HD) for i in range(3)]
        grads = head_grads(pv[:, cols[0]], pv[:, cols[1]], pv[:, cols[2]], gv[:, pl.ds(h * HD, HD)])
        for col, grad in zip(cols, grads):
            gp[:, col] = grad.astype(BF16)
    core.append(remote(gp, gp2, core_s.at[8], core_r.at[8], to_core))

    def block_rows(block, j):
        h = 1 - yh if j == 0 else yh
        return pl.ds(pl.multiple_of(block * 2 * OWN + h * OWN, OWN), OWN)

    def rs_block(way, step):
        return (z + NZ - step - 1) % NZ if way == 0 else (z + step + 1) % NZ

    half = [pl.ds(0, HALF), pl.ds(HALF, HALF)]
    rs = {}

    def rs_send(way, step, j):
        src = (
            tv.at[block_rows(rs_block(way, 0), j), half[way]]
            if step == 0
            else slots.at[way, step - 1, j]
        )
        rs[way, step, j] = remote(
            src, slots.at[way, step, j], rs_s.at[way, step, j], rs_r.at[way, step, j], to_z[way]
        )

    def terms(cols):
        total = dot(gp[:, pl.ds(0, INNER)], wv[0, cols, :], 1, 1)
        for i in range(1, 3):
            total += dot(gp[:, pl.ds(i * INNER, INNER)], wv[i, cols, :], 1, 1)
        tv[:, cols] = total.astype(BF16)

    for way in range(2):
        def body(i, carry, way=way):
            terms(pl.ds(pl.multiple_of(way * HALF + i * 512, 512), 512))
            return carry

        lax.fori_loop(0, HALF // 512, body, 0)
        for j in range(2):
            rs_send(way, 0, j)

    def rs_take(step):
        for j in range(2):
            for way in range(2):
                rs[way, step, j].wait_recv()
                slot = slots.at[way, step, j]
                own = tv[block_rows(rs_block(way, step + 1), j), half[way]]
                slot[...] = (slot[...].astype(F32) + own.astype(F32)).astype(BF16)
                rs_send(way, step + 1, j)

    def b_units(k):
        for way in range(2):
            block = (x + NX - 1 - k) % NX if way == 0 else (x + 1 + k) % NX
            for j in range(2):
                ys = 1 - yl if j == 0 else yl
                mine = pl.ds(pl.multiple_of(((block * 2 + ys) * 2 + c) * SLICE, 128), SLICE)
                other = pl.ds(pl.multiple_of((block * 2 + ys) * SLICE, 128), SLICE)
                e = pl.ds(way * EH, EH)
                total = dot(nv[:, mine], gp[:, e], 0, 0) + dot(nr[:, other], gp2[:, e], 0, 0)
                bp[way, k, j] = total.astype(BF16)

    b = {}

    def b_send(way, step, j):
        src = bp.at[way, 0, j] if step == 0 else rb.at[way, step - 1, j]
        b[way, step, j] = remote(
            src, rb.at[way, step, j], b_s.at[way, step, j], b_r.at[way, step, j], to_x[way]
        )

    def b_sum(way, step, j):
        b[way, step, j].wait_recv()
        return rb[way, step, j].astype(F32) + bp[way, step + 1, j].astype(F32)

    def b_take(step):
        for j in range(2):
            for way in range(2):
                rb[way, step, j] = b_sum(way, step, j).astype(BF16)
                b_send(way, step + 1, j)

    for cp in core:
        cp.wait_recv()
    b_units(0)
    for j in range(2):
        for way in range(2):
            b_send(way, 0, j)
    own_rows = pl.ds(pl.multiple_of(mp * OWN, OWN), OWN)
    hat, inv = normalize(xv[own_rows, :].astype(F32))
    xh[...] = hat
    xinv[...] = jnp.broadcast_to(inv, xinv.shape)
    rs_take(0)
    b_units(1)
    rs_take(1)
    b_units(2)
    rs_take(2)
    b_units(3)
    rs_take(3)
    rs_take(4)
    b_take(0)
    rs_take(5)

    last = NZ - 2
    y = []
    for way in range(2):
        rs[way, last, 0].wait_recv()
        slot = slots.at[way, last, 0]
        own = tv[block_rows(z, 0), half[way]]
        slot[...] = (slot[...].astype(F32) + own.astype(F32)).astype(BF16)
        y.append(remote(slot, ry.at[way], ry_s.at[way], ry_r.at[way], to_yh))
    totals = []
    for way in range(2):
        rs[way, last, 1].wait_recv()
        y[way].wait_recv()
        own = tv[block_rows(z, 1), half[way]]
        totals.append(slots[way, last, 1].astype(F32) + own.astype(F32) + ry[way].astype(F32))
    grad_normed = jnp.concatenate(totals, axis=1)
    og[own_rows, :] = norm_back(grad_normed, xh[...], xinv[:, :1]).astype(BF16)

    ag = {}

    def ag_send(way, step, j):
        block = (z + NZ - step) % NZ if way == 0 else (z + step) % NZ
        part = og.at[block_rows(block, 1 - j), half[way]]
        ag[way, step, j] = remote(
            part, part, ag_s.at[way, step, j], ag_r.at[way, step, j], to_z[way]
        )

    def ag_take(step):
        for j in range(2):
            for way in range(2):
                ag[way, step, j].wait_recv()
                if step < NZ - 2:
                    ag_send(way, step + 1, j)

    ay = remote(og.at[own_rows, :], og.at[own_rows, :], ay_s, ay_r, to_yh)
    for way in range(2):
        ag_send(way, 0, 0)
    ay.wait_recv()
    for way in range(2):
        ag_send(way, 0, 1)
    ag_take(0)
    b_take(1)
    ag_take(1)
    ag_take(2)
    ag_take(3)
    by = []
    for way in range(2):
        rb[way, 2, 0] = b_sum(way, 2, 0).astype(BF16)
        by.append(remote(rb.at[way, 2, 0], yb.at[way], by_s.at[way], by_r.at[way], to_yl))
    ag_take(4)
    ag_take(5)
    for way in range(2):
        total = b_sum(way, 2, 1)
        by[way].wait_recv()
        total = (total + yb[way].astype(F32)).astype(BF16)
        if way == 0:
            gwv[0, :, :] = total[:, :256]
            gwv[1, :, :128] = total[:, 256:]
        else:
            gwv[1, :, 128:] = total[:, :128]
            gwv[2, :, :] = total[:, 128:]
    q_copy = pltpu.make_async_copy(gwv, gw_hbm, q_sem)
    q_copy.start()
    ag_take(6)
    o_copy = pltpu.make_async_copy(og, gi_hbm, o_sem)
    o_copy.start()
    for cp in sends:
        cp.wait_send()
    q_copy.wait()
    o_copy.wait()


def on_device(block_input, qkv_weight, grad_attn):
    dma = pltpu.SemaphoreType.DMA
    return pl.pallas_call(
        kernel,
        out_shape=(
            jax.ShapeDtypeStruct((ROWS, D), BF16),
            jax.ShapeDtypeStruct((3, SLICE, INNER), BF16),
        ),
        in_specs=[pl.BlockSpec(memory_space=pl.ANY)] * 3,
        out_specs=[pl.BlockSpec(memory_space=pl.ANY)] * 2,
        scratch_shapes=[
            pltpu.VMEM((ROWS, D), BF16),
            pltpu.VMEM((3, D, INNER), BF16),
            pltpu.VMEM((ROWS, INNER), BF16),
            pltpu.VMEM((ROWS, D), BF16),
            pltpu.VMEM((ROWS, 3 * INNER), BF16),
            pltpu.VMEM((ROWS, 3 * INNER), BF16),
            pltpu.VMEM((ROWS, 3 * INNER), BF16),
            pltpu.VMEM((ROWS, HALF), BF16),
            pltpu.VMEM((ROWS, D), BF16),
            pltpu.VMEM((2, NZ - 1, 2, OWN, HALF), BF16),
            pltpu.VMEM((2, OWN, HALF), BF16),
            pltpu.VMEM((ROWS, D), BF16),
            pltpu.VMEM((2, NX, 2, SLICE, EH), BF16),
            pltpu.VMEM((2, NX - 1, 2, SLICE, EH), BF16),
            pltpu.VMEM((2, SLICE, EH), BF16),
            pltpu.VMEM((OWN, D), F32),
            pltpu.VMEM((OWN, 128), F32),
            pltpu.VMEM((3, SLICE, INNER), BF16),
            dma((4,)), dma((3,)), dma(()), dma(()), dma(()),
            dma((9,)), dma((9,)),
            dma((2, NZ - 1, 2)), dma((2, NZ - 1, 2)),
            dma((2,)), dma((2,)),
            dma((2, NZ - 1, 2)), dma((2, NZ - 1, 2)),
            dma(()), dma(()),
            dma((2, NX - 1, 2)), dma((2, NX - 1, 2)),
            dma((2,)), dma((2,)),
        ],
        compiler_params=pltpu.CompilerParams(
            collective_id=0, has_side_effects=True, vmem_limit_bytes=56 * 2**20
        ),
        cost_estimate=pl.CostEstimate(flops=7_500_000_000, bytes_accessed=20_000_000, transcendentals=200_000),
    )(block_input, qkv_weight, grad_attn)


def solution(mesh):
    placed = (P("dp", None), P(None, None, "mp"), P("dp", "mp"))
    return jax.shard_map(
        on_device,
        mesh=mesh,
        in_specs=placed,
        out_specs=(P("dp", None), P(None, "dp", "mp")),
        check_vma=False,
    )
```

time: 345 us -> 103 us (0.30)
  waiting for transfers between devices: 231 us -> 0 us
  Pallas kernels: 0 us -> 97 us
  matrix products: 38.9 us -> 0 us
  local copies, waits for them, and re-layouts: 35 us -> 4.76 us
  other arithmetic: 23.4 us -> 0 us
  between operations: 15.6 us -> 0.65 us
    psum x1 -> x0, waiting for transfers between devices: 231 us -> none  [on_device(): lax.psum(input_terms.astype(jnp.bfloat16), 'mp').astype(jnp.float32)]
    pallas_call x0 -> x1, Pallas kernels: none -> 97 us  [on_device(): pl.pallas_call(kernel, out_shape=(jax.ShapeDtypeStruct((ROWS, D), BF16),...]
    dot_general x8 -> x0, matrix products: 36.8 us -> none  [the longest x1 11.1 us: on_device(): jnp.einsum('tce,cde->td', grad_proj, qkv_weight, preferred_element_type=j...]
    unnamed x16 -> x4, local copies, waits for them, and re-layouts: 33 us -> 4.76 us
    reduce_sum x7 -> x0, other arithmetic: 12.1 us -> none  [the longest x3 4.14 us: normalize(): row_mean = jnp.mean(values, axis=-1, keepdims=True)]
    convert_element_type x2 -> x0, other arithmetic: 5.23 us -> none  [the longest x1 3.58 us: on_device(): grad_input = norm_back(grad_normed, x_hat, x_inv).astype(jnp.bfloat16)]
  transfers between devices with their start and end apart: 2 -> 0, of which waited for: 1 -> 0; matrix products, arithmetic and copies ran while one was open for 13% -> 0% of each run, Pallas kernels for 0% -> 0%
where the time goes in v1:
time: 103 us; the launch traced here: 102 us
  Pallas kernels  97 us (94%)
  local copies, waits for them, and re-layouts  4.76 us (5%)
    pallas_call x1, Pallas kernels, on_device(): pl.pallas_call(kernel, out_shape=(jax.ShapeDtypeStruct((ROWS, D), BF16),...  97 us
    unnamed x4, local copies, waits for them, and re-layouts  4.76 us

profile of v1, /device:TPU:14, one launch (start us, length us, event | category | flops | bytes accessed | tf_op | source)
XLA Modules:
  0.0 102.4 jit_solution(7576104030845421935)
XLA Ops:
  0.6 97.0 %shard_map.50 = (bf16[256,6144]{1,0:T(8,128)(2,1)}, bf16[3,384,256]{2,1,0:T(8,128)(2,1)}) custom-call(bf16[256,6144]{1,0:T(8,128)(2,1)} %x_hbm.1, bf16[3,6144,256]{2,1,0:T(8,128)(2,1)} %w_hbm.1, bf16[256,256]{1,0:T(8,128)(2,1)} %g_hbm.1), custom_call_target="tpu_custom_call" | custom-call | flops 7500000256 | bytes 20000000 | tf_op jit(solution)/shard_map/pallas_call | solution.py:295
  97.6 0.0 copy-start
  97.6 3.9 %copy.7 = bf16[256,6144]{1,0:T(8,128)(2,1)} copy(bf16[256,6144]{1,0:T(8,128)(2,1)} %get-tuple-element.4) | data formatting | bytes 6291456
  101.6 0.0 copy-done
  101.6 0.8 copy.8
Async XLA Ops:
  97.6 4.0 %copy-start = (bf16[3,384,256]{2,1,0:T(8,128)(2,1)S(1)}, bf16[3,384,256]{2,1,0:T(8,128)(2,1)}, u32[]{:S(2)}) copy-start(bf16[3,384,256]{2,1,0:T(8,128)(2,1)} %get-tuple-element.5) | copy-start | bytes 1769476

commit v2 on v1

v2 whole, which is shorter than its diff:
```python
import functools
import math

import jax
import jax.numpy as jnp
from jax import lax
from jax.experimental import pallas as pl
from jax.experimental.pallas import tpu as pltpu
from jax.sharding import PartitionSpec as P

MESH = pl.DeviceIdType.MESH
F32 = jnp.float32
BF16 = jnp.bfloat16
EPSILON = 1e-06

NX, NZ = 4, 8
ROWS = 256
D = 6144
HALF = D // 2
INNER = 256
HD = 128
OWN = 16
SLICE = 384
EH = 384
FRAME = ROWS // 2
RZ = 1536
XROWS = 64
TW = 512
AZ = 2048


def normalize(values):
    row_mean = jnp.mean(values, axis=-1, keepdims=True)
    centered = values - row_mean
    inv_std = lax.rsqrt(jnp.mean(centered * centered, axis=-1, keepdims=True) + EPSILON)
    return centered * inv_std, inv_std


def norm_back(upstream, normed, inv_std):
    mean_grad = jnp.mean(upstream, axis=-1, keepdims=True)
    mean_cross = jnp.mean(upstream * normed, axis=-1, keepdims=True)
    return inv_std * (upstream - mean_grad - normed * mean_cross)


def dot(a, b, ca, cb):
    return lax.dot_general(a, b, (((ca,), (cb,)), ((), ())), preferred_element_type=F32)


def head_grads(q, k, v, g):
    factor = 1.0 / math.sqrt(HD)
    q_hat, q_inv = normalize(q.astype(F32))
    k_hat, k_inv = normalize(k.astype(F32))
    q_low = q_hat.astype(BF16)
    k_low = k_hat.astype(BF16)
    exp_scores = jnp.exp(dot(q_low, k_low, 1, 1) * factor)
    probs = exp_scores / jnp.sum(exp_scores, axis=-1, keepdims=True)
    grad_probs = dot(g, v, 1, 1)
    grad_v = dot(probs.astype(BF16), g, 0, 0)
    row_term = jnp.sum(probs * grad_probs, axis=-1, keepdims=True)
    grad_scores = (probs * (grad_probs - row_term) * factor).astype(BF16)
    grad_q = norm_back(dot(grad_scores, k_low, 1, 0), q_hat, q_inv)
    grad_k = norm_back(dot(grad_scores, q_low, 0, 0), k_hat, k_inv)
    return grad_q, grad_k, grad_v


def kernel(
    x_hbm, w_hbm, g_hbm, og, gwv,
    xv, wv, gv, nv, pv, gp, gp2, nr, tv, slots, yx, ry, bp, rb, yb, xh, xinv,
    x_sem, w_sem, g_sem,
    core_s, core_r, rs_s, rs_r, yx_s, yx_r, ry_s, ry_r,
    ag_s, ag_r, ay_s, ay_r, b_s, b_r, by_s, by_r,
):
    dp, mp = lax.axis_index("dp"), lax.axis_index("mp")
    x, yl, c = dp // 4, (dp // 2) % 2, dp % 2
    z, yh = mp // 2, mp % 2

    def at(x_, yl_, c_, z_, yh_):
        return ((x_ * 2 + yl_) * 2 + c_, z_ * 2 + yh_)

    to_z = (at(x, yl, c, (z + 1) % NZ, yh), at(x, yl, c, (z + NZ - 1) % NZ, yh))
    to_x = (at((x + 1) % NX, yl, c, z, yh), at((x + NX - 1) % NX, yl, c, z, yh))
    to_yh = at(x, yl, c, z, 1 - yh)
    to_yl = at(x, 1 - yl, c, z, yh)
    to_core = at(x, yl, 1 - c, z, yh)

    def x_copy(i):
        rows = pl.ds(pl.multiple_of(i * XROWS, XROWS), XROWS)
        return pltpu.make_async_copy(x_hbm.at[rows], xv.at[rows], x_sem.at[i])

    def w_copy(i):
        return pltpu.make_async_copy(w_hbm.at[i], wv.at[i], w_sem.at[i])

    g_copy = pltpu.make_async_copy(g_hbm, gv, g_sem)
    for i in range(ROWS // XROWS):
        x_copy(i).start()
    for i in range(3):
        w_copy(i).start()
    g_copy.start()

    barrier = pltpu.get_barrier_semaphore()
    neighbours = to_z + to_x + (to_yh, to_yl, to_core)
    for d in neighbours:
        pl.semaphore_signal(barrier, inc=1, device_id=d, device_id_type=MESH)

    sends = []

    def remote(src, dst, s, r, d):
        cp = pltpu.make_async_remote_copy(
            src_ref=src, dst_ref=dst, send_sem=s, recv_sem=r, device_id=d, device_id_type=MESH
        )
        cp.start()
        sends.append(cp)
        return cp

    def loop(count, step):
        def body(i, carry):
            step(i)
            return carry

        lax.fori_loop(0, count, body, 0)

    def normed_rows(i):
        x_copy(i).wait()
        rows = pl.ds(pl.multiple_of(i * XROWS, XROWS), XROWS)
        shape = (XROWS, 128)
        tiles = [pl.ds(t * 128, 128) for t in range(D // 128)]
        total = jnp.zeros(shape, F32)
        for tile in tiles:
            total += xv[rows, tile].astype(F32)
        mean = jnp.broadcast_to(jnp.sum(total, axis=-1, keepdims=True) * (1.0 / D), shape)
        total = jnp.zeros(shape, F32)
        for tile in tiles:
            centered = xv[rows, tile].astype(F32) - mean
            total += centered * centered
        variance = jnp.sum(total, axis=-1, keepdims=True) * (1.0 / D)
        inv = jnp.broadcast_to(lax.rsqrt(variance + EPSILON), shape)
        for tile in tiles:
            nv[rows, tile] = ((xv[rows, tile].astype(F32) - mean) * inv).astype(BF16)

    loop(ROWS // XROWS, normed_rows)
    pl.semaphore_wait(barrier, len(neighbours))
    core = []
    for i in range(8):
        cols = pl.ds(pl.multiple_of((i * 2 + 1 - c) * SLICE, 128), SLICE)
        core.append(
            remote(nv.at[:, cols], nr.at[:, pl.ds(i * SLICE, SLICE)], core_s.at[i], core_r.at[i], to_core)
        )

    def project(i):
        w_copy(i).wait()
        pv[:, pl.ds(pl.multiple_of(i * INNER, INNER), INNER)] = dot(nv[...], wv[i], 1, 0).astype(BF16)

    loop(3, project)
    g_copy.wait()

    def head(h):
        start = pl.multiple_of(h * HD, HD)
        cols = [pl.ds(i * INNER + start, HD) for i in range(3)]
        grads = head_grads(pv[:, cols[0]], pv[:, cols[1]], pv[:, cols[2]], gv[:, pl.ds(start, HD)])
        for col, grad in zip(cols, grads):
            gp[:, col] = grad.astype(BF16)

    loop(INNER // HD, head)
    core.append(remote(gp, gp2, core_s.at[8], core_r.at[8], to_core))

    chains = [(way, ch) for ch in range(2) for way in range(2)]

    def hops(way, ch):
        return NZ // 2 if way == ch else NZ // 2 - 1

    def block_rows(block, h):
        return pl.ds(pl.multiple_of(h * FRAME + block * OWN, OWN), OWN)

    def ahead(way, far):
        return far if way == 0 else (NZ - far) % NZ

    rs_cols = [[pl.ds(ch * HALF, RZ)] * 2 + [pl.ds(ch * HALF + RZ, HALF - RZ)] for ch in range(2)]
    rs, y_first = {}, {}

    def rs_part(ch, delta, u, h):
        return tv.at[block_rows((z + delta) % NZ, h), rs_cols[ch][u]]

    def rs_own(ch, delta, u):
        own = rs_part(ch, delta, u, 1 - yh if u == 0 else yh)[...].astype(F32)
        if u == 2:
            y_first[ch, delta].wait_recv()
            own += yx[ch, delta].astype(F32)
        return own

    def rs_send(way, ch, k, u, src):
        rs[way, ch, k, u] = remote(
            src, slots.at[way, ch, k, u], rs_s.at[way, ch, k, u], rs_r.at[way, ch, k, u], to_z[way]
        )

    def rs_start(ch, u):
        for way in range(2):
            delta = ahead(way, hops(way, ch))
            if u == 2:
                yx[ch, delta] = rs_own(ch, delta, u).astype(BF16)
                src = yx.at[ch, delta]
            else:
                src = rs_part(ch, delta, u, 1 - yh if u == 0 else yh)
            rs_send(way, ch, 0, u, src)

    def rs_take(k, u):
        for way, ch in chains:
            far = hops(way, ch) - k - 1
            if far > 0:
                own = rs_own(ch, ahead(way, far), u)
                rs[way, ch, k, u].wait_recv()
                slots[way, ch, k, u] = (slots[way, ch, k, u].astype(F32) + own).astype(BF16)
                rs_send(way, ch, k + 1, u, slots.at[way, ch, k, u])

    def rs_total(ch, u):
        total = rs_own(ch, 0, u)
        for way in (1 - ch, ch):
            k = hops(way, ch) - 1
            rs[way, ch, k, u].wait_recv()
            total += slots[way, ch, k, u].astype(F32)
        return total

    def terms(start, width):
        def part(i):
            cols = pl.ds(pl.multiple_of(start + i * TW, TW), TW)
            total = dot(gp[:, pl.ds(0, INNER)], wv[0, cols, :], 1, 1)
            for j in range(1, 3):
                total += dot(gp[:, pl.ds(j * INNER, INNER)], wv[j, cols, :], 1, 1)
            tv[:, cols] = total.astype(BF16)

        loop(width // TW, part)

    for ch in range(2):
        terms(ch * HALF, RZ)
        for u in range(2):
            rs_start(ch, u)
    for ch in range(2):
        terms(ch * HALF + RZ, HALF - RZ)
    for delta in (4, 3, 5, 2, 6, 1, 7, 0):
        for ch in range(2):
            y_first[ch, delta] = remote(
                rs_part(ch, delta, 2, 1 - yh), yx.at[ch, delta], yx_s.at[ch, delta], yx_r.at[ch, delta], to_yh
            )

    def b_units(j):
        ys = 1 - yl if j == 0 else yl

        def unit(delta):
            block = (x + delta) % NX
            mine = pl.ds(pl.multiple_of(((block * 2 + ys) * 2 + c) * SLICE, 128), SLICE)
            other = pl.ds(pl.multiple_of((block * 2 + ys) * SLICE, 128), SLICE)
            total = dot(nv[:, mine], gp[...], 0, 0) + dot(nr[:, other], gp2[...], 0, 0)
            for ch in range(2):
                bp[j, delta, ch] = total[:, ch * EH : (ch + 1) * EH].astype(BF16)

        loop(NX, unit)

    b = {}

    def b_send(way, ch, k, j, src):
        b[way, ch, k, j] = remote(
            src, rb.at[way, ch, k, j], b_s.at[way, ch, k, j], b_r.at[way, ch, k, j], to_x[way]
        )

    def b_start(j):
        for way in range(2):
            b_send(way, way, 0, j, bp.at[j, 2, way])
        for way in range(2):
            b_send(way, 1 - way, 0, j, bp.at[j, 1 if way == 0 else 3, 1 - way])

    def b_take(j):
        for way in range(2):
            b[way, way, 0, j].wait_recv()
            own = bp[j, 1 if way == 0 else 3, way].astype(F32)
            rb[way, way, 0, j] = (rb[way, way, 0, j].astype(F32) + own).astype(BF16)
            b_send(way, way, 1, j, rb.at[way, way, 0, j])

    def b_total(ch, j):
        b[1 - ch, ch, 0, j].wait_recv()
        b[ch, ch, 1, j].wait_recv()
        total = bp[j, 0, ch].astype(F32) + rb[1 - ch, ch, 0, j].astype(F32)
        return total + rb[ch, ch, 1, j].astype(F32)

    for cp in core:
        cp.wait_recv()
    b_units(0)
    b_start(0)
    own_rows = block_rows(z, yh)
    hat, inv = normalize(xv[own_rows, :].astype(F32))
    xh[...] = hat
    xinv[...] = jnp.broadcast_to(inv, xinv.shape)
    rs_take(0, 0)
    rs_take(0, 1)
    for ch in range(2):
        rs_start(ch, 2)
    b_units(1)
    rs_take(1, 0)
    rs_take(1, 1)
    rs_take(0, 2)
    b_take(0)
    b_start(1)
    rs_take(2, 0)
    rs_take(2, 1)
    rs_take(1, 2)
    y = []
    for ch in range(2):
        slots[ch, ch, 3, 0] = rs_total(ch, 0).astype(BF16)
        y.append(remote(slots.at[ch, ch, 3, 0], ry.at[ch], ry_s.at[ch], ry_r.at[ch], to_yh))
    rs_take(2, 2)
    totals = [[rs_total(ch, 1)] for ch in range(2)]
    for ch in range(2):
        totals[ch].append(rs_total(ch, 2))
    for ch in range(2):
        y[ch].wait_recv()
        totals[ch][0] += ry[ch].astype(F32)
    grad_normed = jnp.concatenate(totals[0] + totals[1], axis=1)
    og[own_rows, :] = norm_back(grad_normed, xh[...], xinv[:, :1]).astype(BF16)

    ag, ay = {}, {}
    ag_cols = [[pl.ds(ch * HALF, HALF), pl.ds(ch * HALF, AZ)] for ch in range(2)]
    y_cols = [pl.ds(ch * HALF + AZ, HALF - AZ) for ch in range(2)]

    def ag_send(way, ch, k, u):
        block = (z + ahead(1 - way, k)) % NZ
        part = og.at[block_rows(block, yh if u == 0 else 1 - yh), ag_cols[ch][u]]
        ag[way, ch, k, u] = remote(
            part, part, ag_s.at[way, ch, k, u], ag_r.at[way, ch, k, u], to_z[way]
        )

    def y_send(ch, delta, cols, i):
        part = og.at[block_rows((z + delta) % NZ, yh), cols]
        ay[ch, i] = remote(part, part, ay_s.at[ch, i], ay_r.at[ch, i], to_yh)

    def ag_take(k):
        for u in range(2):
            for way, ch in ((0, 0), (1, 1), (1, 0), (0, 1)):
                if k < hops(way, ch):
                    ag[way, ch, k, u].wait_recv()
                    if k + 1 < hops(way, ch):
                        ag_send(way, ch, k + 1, u)
                    if u == 0:
                        delta = ahead(1 - way, k + 1)
                        y_send(ch, delta, y_cols[ch], delta)

    for ch in range(2):
        y_send(ch, 0, ag_cols[ch][1], NZ)
    for ch in range(2):
        for way in range(2):
            ag_send(way, ch, 0, 0)
    for ch in range(2):
        y_send(ch, 0, y_cols[ch], 0)
    for ch in range(2):
        ay[ch, NZ].wait_recv()
        for way in range(2):
            ag_send(way, ch, 0, 1)
    by = []
    for ch in range(2):
        rb[ch, ch, 1, 0] = b_total(ch, 0).astype(BF16)
        by.append(remote(rb.at[ch, ch, 1, 0], yb.at[ch], by_s.at[ch], by_r.at[ch], to_yl))
    ag_take(0)
    b_take(1)
    ag_take(1)
    ag_take(2)
    for ch in range(2):
        total = b_total(ch, 1)
        by[ch].wait_recv()
        total = (total + yb[ch].astype(F32)).astype(BF16)
        if ch == 0:
            gwv[0, :, :] = total[:, :256]
            gwv[1, :, :128] = total[:, 256:]
        else:
            gwv[1, :, 128:] = total[:, :128]
            gwv[2, :, :] = total[:, 128:]
    ag_take(3)
    for i in range(NZ):
        for ch in range(2):
            ay[ch, i].wait_recv()
    for cp in sends:
        cp.wait_send()


def on_device(block_input, qkv_weight, grad_attn):
    dma = pltpu.SemaphoreType.DMA
    vmem = pl.BlockSpec(memory_space=pltpu.VMEM)
    return pl.pallas_call(
        kernel,
        out_shape=(pltpu.VMEM((ROWS, D), BF16), pltpu.VMEM((3, SLICE, INNER), BF16)),
        in_specs=[pl.BlockSpec(memory_space=pl.ANY)] * 3,
        out_specs=(vmem, vmem),
        scratch_shapes=[
            pltpu.VMEM((ROWS, D), BF16),
            pltpu.VMEM((3, D, INNER), BF16),
            pltpu.VMEM((ROWS, INNER), BF16),
            pltpu.VMEM((ROWS, D), BF16),
            pltpu.VMEM((ROWS, 3 * INNER), BF16),
            pltpu.VMEM((ROWS, 3 * INNER), BF16),
            pltpu.VMEM((ROWS, 3 * INNER), BF16),
            pltpu.VMEM((ROWS, HALF), BF16),
            pltpu.VMEM((ROWS, D), BF16),
            pltpu.VMEM((2, 2, NZ // 2, 3, OWN, RZ), BF16),
            pltpu.VMEM((2, NZ, OWN, HALF - RZ), BF16),
            pltpu.VMEM((2, OWN, RZ), BF16),
            pltpu.VMEM((2, NX, 2, SLICE, EH), BF16),
            pltpu.VMEM((2, 2, 2, 2, SLICE, EH), BF16),
            pltpu.VMEM((2, SLICE, EH), BF16),
            pltpu.VMEM((OWN, D), F32),
            pltpu.VMEM((OWN, 128), F32),
            dma((ROWS // XROWS,)), dma((3,)), dma(()),
            dma((9,)), dma((9,)),
            dma((2, 2, NZ // 2, 3)), dma((2, 2, NZ // 2, 3)),
            dma((2, NZ)), dma((2, NZ)),
            dma((2,)), dma((2,)),
            dma((2, 2, NZ // 2, 2)), dma((2, 2, NZ // 2, 2)),
            dma((2, NZ + 1)), dma((2, NZ + 1)),
            dma((2, 2, 2, 2)), dma((2, 2, 2, 2)),
            dma((2,)), dma((2,)),
        ],
        compiler_params=pltpu.CompilerParams(
            collective_id=0, has_side_effects=True, vmem_limit_bytes=54 * 2**20
        ),
        cost_estimate=pl.CostEstimate(flops=7_500_000_000, bytes_accessed=20_000_000, transcendentals=200_000),
    )(block_input, qkv_weight, grad_attn)


def solution(mesh):
    placed = (P("dp", None), P(None, None, "mp"), P("dp", "mp"))
    return jax.shard_map(
        on_device,
        mesh=mesh,
        in_specs=placed,
        out_specs=(P("dp", None), P(None, "dp", "mp")),
        check_vma=False,
    )
```

time: 103 us -> 80.8 us (0.78)
  Pallas kernels: 97 us -> 76.9 us
  local copies, waits for them, and re-layouts: 4.76 us -> 2.48 us
    pallas_call x1, Pallas kernels: 97 us -> 76.9 us  [on_device(): pl.pallas_call(kernel, out_shape=(pltpu.VMEM((ROWS, D), BF16), pltpu.VMEM...]
    unnamed x4 -> x2, local copies, waits for them, and re-layouts: 4.76 us -> 2.48 us
where the time goes in v2:
time: 80.8 us; the launch traced here: 80 us
  Pallas kernels  76.9 us (95%)
  local copies, waits for them, and re-layouts  2.48 us (3%)
    pallas_call x1, Pallas kernels, on_device(): pl.pallas_call(kernel, out_shape=(pltpu.VMEM((ROWS, D), BF16), pltpu.VMEM...  76.9 us
    unnamed x2, local copies, waits for them, and re-layouts  2.48 us

profile of v2, /device:TPU:14, one launch (start us, length us, event | category | flops | bytes accessed | tf_op | source)
XLA Modules:
  0.0 80.0 jit_solution(5446490559863646575)
XLA Ops:
  0.6 76.9 %shard_map.50 = (bf16[256,6144]{1,0:T(8,128)(2,1)S(1)}, bf16[3,384,256]{2,1,0:T(8,128)(2,1)S(1)}) custom-call(bf16[256,6144]{1,0:T(8,128)(2,1)} %x_hbm.1, bf16[3,6144,256]{2,1,0:T(8,128)(2,1)} %w_hbm.1, bf16[256,256]{1,0:T(8,128)(2,1)} %g_hbm.1), custom_call_target="tpu_custom_call" | custom-call | flops 7500000256 | bytes 20000000 | tf_op jit(solution)/shard_map/pallas_call | solution.py:384
  77.5 1.7 %copy.7 = bf16[256,6144]{1,0:T(8,128)(2,1)} copy(bf16[256,6144]{1,0:T(8,128)(2,1)S(1)} %get-tuple-element.2) | data formatting | bytes 6291456
  79.2 0.8 %copy.8 = bf16[3,384,256]{2,1,0:T(8,128)(2,1)} copy(bf16[3,384,256]{2,1,0:T(8,128)(2,1)S(1)} %get-tuple-element.3) | data formatting | bytes 1179648

commit v3 on v2

v3 whole, which is shorter than its diff:
```python
import functools
import math

import jax
import jax.numpy as jnp
from jax import lax
from jax.experimental import pallas as pl
from jax.experimental.pallas import tpu as pltpu
from jax.sharding import PartitionSpec as P

MESH = pl.DeviceIdType.MESH
F32 = jnp.float32
BF16 = jnp.bfloat16
EPSILON = 1e-06

NX, NZ = 4, 8
ROWS = 256
D = 6144
HALF = D // 2
INNER = 256
HD = 128
OWN = 16
SLICE = 384
EH = 384
XROWS = 64
RZ = 1280
RY = HALF - RZ
AZ = 2048
AY = HALF - AZ
CHAINS = ((0, 0), (1, 1), (1, 0), (0, 1))
HOPS = {chain: 4 if chain[0] == chain[1] else 3 for chain in CHAINS}
FIRST = {(0, 0): 0, (1, 1): 4, (1, 0): 8, (0, 1): 11}
SLOTS = 14


def normalize(values):
    row_mean = jnp.mean(values, axis=-1, keepdims=True)
    centered = values - row_mean
    inv_std = lax.rsqrt(jnp.mean(centered * centered, axis=-1, keepdims=True) + EPSILON)
    return centered * inv_std, inv_std


def norm_back(upstream, normed, inv_std):
    mean_grad = jnp.mean(upstream, axis=-1, keepdims=True)
    mean_cross = jnp.mean(upstream * normed, axis=-1, keepdims=True)
    return inv_std * (upstream - mean_grad - normed * mean_cross)


def dot(a, b, ca, cb):
    return lax.dot_general(a, b, (((ca,), (cb,)), ((), ())), preferred_element_type=F32)


def head_grads(q, k, v, g):
    factor = 1.0 / math.sqrt(HD)
    q_hat, q_inv = normalize(q.astype(F32))
    k_hat, k_inv = normalize(k.astype(F32))
    q_low = q_hat.astype(BF16)
    k_low = k_hat.astype(BF16)
    exp_scores = jnp.exp(dot(q_low, k_low, 1, 1) * factor)
    probs = exp_scores / jnp.sum(exp_scores, axis=-1, keepdims=True)
    grad_probs = dot(g, v, 1, 1)
    grad_v = dot(probs.astype(BF16), g, 0, 0)
    row_term = jnp.sum(probs * grad_probs, axis=-1, keepdims=True)
    grad_scores = (probs * (grad_probs - row_term) * factor).astype(BF16)
    grad_q = norm_back(dot(grad_scores, k_low, 1, 0), q_hat, q_inv)
    grad_k = norm_back(dot(grad_scores, q_low, 0, 0), k_hat, k_inv)
    return grad_q, grad_k, grad_v


def kernel(
    x_hbm, w_hbm, g_hbm, og, gwv,
    xv, wv, gv, nv, pv, gp, gp2, nr, tv, zslots, yslots, yx, zf, ry, bp, rb, yb, xh, xinv,
    x_sem, w_sem, g_sem, s_sem, core_sem, z_sem, y_sem, yx_sem, ry_sem, ag_sem, az_sem, ay_sem, b_sem, by_sem,
):
    dp, mp = lax.axis_index("dp"), lax.axis_index("mp")
    x, yl, c = dp // 4, (dp // 2) % 2, dp % 2
    z, yh = mp // 2, mp % 2

    def at(x_, yl_, c_, z_, yh_):
        return ((x_ * 2 + yl_) * 2 + c_, z_ * 2 + yh_)

    to_z = (at(x, yl, c, (z + 1) % NZ, yh), at(x, yl, c, (z + NZ - 1) % NZ, yh))
    to_x = (at((x + 1) % NX, yl, c, z, yh), at((x + NX - 1) % NX, yl, c, z, yh))
    to_yh = at(x, yl, c, z, 1 - yh)
    to_yl = at(x, 1 - yl, c, z, yh)
    to_core = at(x, yl, 1 - c, z, yh)

    def x_copy(i):
        rows = pl.ds(pl.multiple_of(i * XROWS, XROWS), XROWS)
        return pltpu.make_async_copy(x_hbm.at[rows], xv.at[rows], x_sem.at[i])

    def w_copy(i):
        return pltpu.make_async_copy(w_hbm.at[i], wv.at[i], w_sem.at[i])

    g_copy = pltpu.make_async_copy(g_hbm, gv, g_sem)
    for i in range(ROWS // XROWS):
        x_copy(i).start()
    w_copy(0).start()
    g_copy.start()

    barrier = pltpu.get_barrier_semaphore()
    neighbours = to_z + to_x + (to_yh, to_yl, to_core)
    for d in neighbours:
        pl.semaphore_signal(barrier, inc=1, device_id=d, device_id_type=MESH)

    sent = [0] * 5

    def remote(src, dst, group, r, d):
        cp = pltpu.make_async_remote_copy(
            src_ref=src, dst_ref=dst, send_sem=s_sem.at[group], recv_sem=r, device_id=d, device_id_type=MESH
        )
        cp.start()
        sent[group] += math.prod(src.shape)
        return cp

    def wait_all(ref, sem):
        pltpu.make_async_copy(ref, ref, sem).wait()

    def normed_rows(i, carry):
        x_copy(i).wait()

        @pl.when(i % 2 == 1)
        def _():
            w_copy((i + 1) // 2).start()

        rows = pl.ds(pl.multiple_of(i * XROWS, XROWS), XROWS)
        shape = (XROWS, 128)
        tiles = [pl.ds(t * 128, 128) for t in range(D // 128)]
        total = jnp.zeros(shape, F32)
        for tile in tiles:
            total += xv[rows, tile].astype(F32)
        mean = jnp.broadcast_to(jnp.sum(total, axis=-1, keepdims=True) * (1.0 / D), shape)
        total = jnp.zeros(shape, F32)
        for tile in tiles:
            centered = xv[rows, tile].astype(F32) - mean
            total += centered * centered
        variance = jnp.sum(total, axis=-1, keepdims=True) * (1.0 / D)
        inv = jnp.broadcast_to(lax.rsqrt(variance + EPSILON), shape)
        for tile in tiles:
            nv[rows, tile] = ((xv[rows, tile].astype(F32) - mean) * inv).astype(BF16)
        return carry

    lax.fori_loop(0, ROWS // XROWS, normed_rows, 0)

    def project(i, carry):
        w_copy(i).wait()
        pv[:, pl.ds(pl.multiple_of(i * INNER, INNER), INNER)] = dot(nv[...], wv[i], 1, 0).astype(BF16)
        return carry

    lax.fori_loop(0, 3, project, 0)
    g_copy.wait()
    for h in range(INNER // HD):
        cols = [pl.ds(i * INNER + h * HD, HD) for i in range(3)]
        grads = head_grads(pv[:, cols[0]], pv[:, cols[1]], pv[:, cols[2]], gv[:, pl.ds(h * HD, HD)])
        for col, grad in zip(cols, grads):
            gp[:, col] = grad.astype(BF16)
    pl.semaphore_wait(barrier, len(neighbours))

    def block_rows(delta, h):
        return pl.ds(pl.multiple_of((z + delta) % NZ * 2 * OWN + h * OWN, OWN), OWN)

    def both_rows(delta):
        return pl.ds(pl.multiple_of((z + delta) % NZ * 2 * OWN, 2 * OWN), 2 * OWN)

    def ahead(way, far):
        return far if way == 0 else (NZ - far) % NZ

    rz_cols = (pl.ds(0, RZ), pl.ds(D - RZ, RZ))
    ry_cols = (pl.ds(RZ, RY), pl.ds(HALF, RY))
    ry_part = (pl.ds(0, RY), pl.ds(RY, RY))
    zs, ys, y_first = {}, {}, {}

    def z_send(chain, k, src):
        slot = FIRST[chain] + k
        zs[chain, k] = remote(src, zslots.at[slot], 0, z_sem.at[slot], to_z[chain[0]])

    def y_send(chain, k, src):
        slot = FIRST[chain] + k
        ys[chain, k] = remote(src, yslots.at[slot], 0, y_sem.at[slot], to_z[chain[0]])

    def z_start(ch):
        for way in range(2):
            chain = (way, ch)
            z_send(chain, 0, tv.at[both_rows(ahead(way, HOPS[chain])), rz_cols[ch]])

    def z_take(k):
        for chain in CHAINS:
            way, ch = chain
            far = HOPS[chain] - k - 1
            if far > 0:
                slot = FIRST[chain] + k
                own = tv[both_rows(ahead(way, far)), rz_cols[ch]].astype(F32)
                zs[chain, k].wait_recv()
                zslots[slot] = (zslots[slot].astype(F32) + own).astype(BF16)
                z_send(chain, k + 1, zslots.at[slot])

    def z_total(ch, h):
        rows = pl.ds(pl.multiple_of(h * OWN, OWN), OWN)
        total = tv[block_rows(0, h), rz_cols[ch]].astype(F32)
        for way in (1 - ch, ch):
            slot = FIRST[way, ch] + HOPS[way, ch] - 1
            total += zslots[slot, rows, :].astype(F32)
        return total

    def y_own(ch, delta):
        own = tv[block_rows(delta, yh), ry_cols[ch]].astype(F32)
        return own + yx[delta, :, ry_part[ch]].astype(F32)

    def y_start():
        for delta in (4, 3, 5):
            y_first[delta].wait_recv()
        for chain in CHAINS:
            way, ch = chain
            delta = ahead(way, HOPS[chain])
            yx[delta, :, ry_part[ch]] = y_own(ch, delta).astype(BF16)
            y_send(chain, 0, yx.at[delta, :, ry_part[ch]])

    def y_take(k):
        for way in range(2):
            far = HOPS[1 - way, way] - k - 1
            if far > 0:
                y_first[ahead(way, far)].wait_recv()
        for chain in CHAINS:
            way, ch = chain
            far = HOPS[chain] - k - 1
            if far > 0:
                slot = FIRST[chain] + k
                own = y_own(ch, ahead(way, far))
                ys[chain, k].wait_recv()
                yslots[slot] = (yslots[slot].astype(F32) + own).astype(BF16)
                y_send(chain, k + 1, yslots.at[slot])

    def y_total(ch):
        total = y_own(ch, 0)
        for way in (1 - ch, ch):
            k = HOPS[way, ch] - 1
            ys[(way, ch), k].wait_recv()
            total += yslots[FIRST[way, ch] + k].astype(F32)
        return total

    def terms(start, width):
        cols = pl.ds(start, width)
        total = dot(gp[:, pl.ds(0, INNER)], wv[0, cols, :], 1, 1)
        for j in range(1, 3):
            total += dot(gp[:, pl.ds(j * INNER, INNER)], wv[j, cols, :], 1, 1)
        tv[:, cols] = total.astype(BF16)

    def y_exchange():
        for delta in (4, 3, 5, 2, 6, 1, 7, 0):
            y_first[delta] = remote(
                tv.at[block_rows(delta, 1 - yh), pl.ds(RZ, 2 * RY)], yx.at[delta], 0, yx_sem.at[delta], to_yh
            )

    terms(0, RZ)
    z_start(0)
    terms(D - RZ, RZ)
    z_start(1)
    terms(RZ, RY)
    terms(HALF, RY)
    y_exchange()
    for i in range(8):
        cols = pl.ds(pl.multiple_of((i * 2 + 1 - c) * SLICE, 128), SLICE)
        remote(nv.at[:, cols], nr.at[:, pl.ds(i * SLICE, SLICE)], 2, core_sem.at[0], to_core)
    remote(gp, gp2, 2, core_sem.at[1], to_core)

    def b_units(j):
        ys_ = 1 - yl if j == 0 else yl

        def unit(delta, carry):
            block = (x + delta) % NX
            mine = pl.ds(pl.multiple_of(((block * 2 + ys_) * 2 + c) * SLICE, 128), SLICE)
            other = pl.ds(pl.multiple_of((block * 2 + ys_) * SLICE, 128), SLICE)
            total = dot(nv[:, mine], gp[...], 0, 0) + dot(nr[:, other], gp2[...], 0, 0)
            for ch in range(2):
                bp[j, delta, ch] = total[:, ch * EH : (ch + 1) * EH].astype(BF16)
            return carry

        lax.fori_loop(0, NX, unit, 0)

    def b_send(way, kind, j, src):
        remote(src, rb.at[j, kind, way], 3 + j, b_sem.at[j, 0 if kind == 0 else 1], to_x[way])

    def b_start(j):
        for way in range(2):
            b_send(way, 0, j, bp.at[j, 2, way])
        for way in range(2):
            b_send(way, 1, j, bp.at[j, 1 if way == 0 else 3, 1 - way])

    def b_take(j):
        wait_all(rb.at[j, 0], b_sem.at[j, 0])
        for way in range(2):
            own = bp[j, 1 if way == 0 else 3, way].astype(F32)
            rb[j, 0, way] = (rb[j, 0, way].astype(F32) + own).astype(BF16)
            b_send(way, 2, j, rb.at[j, 0, way])

    def b_total(ch, j):
        total = bp[j, 0, ch].astype(F32) + rb[j, 1, 1 - ch].astype(F32)
        return total + rb[j, 2, ch].astype(F32)

    own_rows = block_rows(0, yh)
    hat, inv = normalize(xv[own_rows, :].astype(F32))
    xh[...] = hat
    xinv[...] = jnp.broadcast_to(inv, xinv.shape)
    wait_all(nr, core_sem.at[0])
    wait_all(gp2, core_sem.at[1])
    b_units(0)
    b_start(0)
    z_take(0)
    y_start()
    b_units(1)
    z_take(1)
    y_take(0)
    b_take(0)
    b_start(1)
    z_take(2)
    y_take(1)
    for chain in CHAINS:
        zs[chain, HOPS[chain] - 1].wait_recv()
    for ch in range(2):
        zf[:, pl.ds(ch * RZ, RZ)] = z_total(ch, 1 - yh).astype(BF16)
    y = remote(zf, ry, 0, ry_sem, to_yh)
    y_take(2)
    totals = [[z_total(ch, yh)] for ch in range(2)]
    y_first[0].wait_recv()
    for ch in range(2):
        totals[ch].append(y_total(ch))
    y.wait_recv()
    for ch in range(2):
        totals[ch][0] += ry[:, pl.ds(ch * RZ, RZ)].astype(F32)
    grad_normed = jnp.concatenate(totals[0] + totals[1][::-1], axis=1)
    og[own_rows, :] = norm_back(grad_normed, xh[...], xinv[:, :1]).astype(BF16)

    ag, az = {}, {}
    ag_cols = ((pl.ds(0, HALF), pl.ds(0, AZ)), (pl.ds(HALF, HALF), pl.ds(D - AZ, AZ)))
    ay_cols = pl.ds(AZ, 2 * AY)

    def ag_send(chain, k, u):
        way, ch = chain
        part = og.at[block_rows(ahead(1 - way, k), yh if u == 0 else 1 - yh), ag_cols[ch][u]]
        ag[chain, k, u] = remote(part, part, 1, ag_sem.at[u, FIRST[chain] + k], to_z[way])

    def ay_send(delta):
        part = og.at[block_rows(delta, yh), ay_cols]
        remote(part, part, 1, ay_sem, to_yh)

    def ag_take(k):
        for u in range(2):
            for chain in CHAINS:
                if k < HOPS[chain]:
                    ag[chain, k, u].wait_recv()
                    if k + 1 < HOPS[chain]:
                        ag_send(chain, k + 1, u)
            if u == 0:
                for delta in {ahead(1 - way, k + 1) for way in range(2)}:
                    ay_send(delta)

    for ch in range(2):
        part = og.at[own_rows, ag_cols[ch][1]]
        az[ch] = remote(part, part, 1, az_sem.at[ch], to_yh)
    for chain in CHAINS:
        ag_send(chain, 0, 0)
    ay_send(0)
    for ch in range(2):
        az[ch].wait_recv()
        for way in range(2):
            ag_send((way, ch), 0, 1)
    wait_all(rb.at[0, pl.ds(1, 2)], b_sem.at[0, 1])
    for ch in range(2):
        rb[0, 2, ch] = b_total(ch, 0).astype(BF16)
    by = remote(rb.at[0, 2], yb, 3, by_sem, to_yl)
    ag_take(0)
    b_take(1)
    ag_take(1)
    ag_take(2)
    wait_all(rb.at[1, pl.ds(1, 2)], b_sem.at[1, 1])
    by.wait_recv()
    for ch in range(2):
        total = (b_total(ch, 1) + yb[ch].astype(F32)).astype(BF16)
        if ch == 0:
            gwv[0, :, :] = total[:, :256]
            gwv[1, :, :128] = total[:, 256:]
        else:
            gwv[1, :, 128:] = total[:, :128]
            gwv[2, :, :] = total[:, 128:]
    ag_take(3)
    wait_all(og.at[pl.ds(0, ROWS // 2), ay_cols], ay_sem)
    for group, count in enumerate(sent):
        wait_all(wv.at[0, pl.ds(0, count // INNER)], s_sem.at[group])


def on_device(block_input, qkv_weight, grad_attn):
    dma = pltpu.SemaphoreType.DMA
    vmem = pl.BlockSpec(memory_space=pltpu.VMEM)
    return pl.pallas_call(
        kernel,
        out_shape=(pltpu.VMEM((ROWS, D), BF16), pltpu.VMEM((3, SLICE, INNER), BF16)),
        in_specs=[pl.BlockSpec(memory_space=pl.ANY)] * 3,
        out_specs=(vmem, vmem),
        scratch_shapes=[
            pltpu.VMEM((ROWS, D), BF16),
            pltpu.VMEM((3, D, INNER), BF16),
            pltpu.VMEM((ROWS, INNER), BF16),
            pltpu.VMEM((ROWS, D), BF16),
            pltpu.VMEM((ROWS, 3 * INNER), BF16),
            pltpu.VMEM((ROWS, 3 * INNER), BF16),
            pltpu.VMEM((ROWS, 3 * INNER), BF16),
            pltpu.VMEM((ROWS, HALF), BF16),
            pltpu.VMEM((ROWS, D), BF16),
            pltpu.VMEM((SLOTS, 2 * OWN, RZ), BF16),
            pltpu.VMEM((SLOTS, OWN, RY), BF16),
            pltpu.VMEM((NZ, OWN, 2 * RY), BF16),
            pltpu.VMEM((OWN, 2 * RZ), BF16),
            pltpu.VMEM((OWN, 2 * RZ), BF16),
            pltpu.VMEM((2, NX, 2, SLICE, EH), BF16),
            pltpu.VMEM((2, 3, 2, SLICE, EH), BF16),
            pltpu.VMEM((2, SLICE, EH), BF16),
            pltpu.VMEM((OWN, D), F32),
            pltpu.VMEM((OWN, 128), F32),
            dma((ROWS // XROWS,)), dma((3,)), dma(()), dma((5,)),
            dma((2,)), dma((SLOTS,)), dma((SLOTS,)), dma((NZ,)), dma(()),
            dma((2, SLOTS)), dma((2,)), dma(()), dma((2, 2)), dma(()),
        ],
        compiler_params=pltpu.CompilerParams(
            collective_id=0, has_side_effects=True, vmem_limit_bytes=54 * 2**20
        ),
        cost_estimate=pl.CostEstimate(flops=7_500_000_000, bytes_accessed=20_000_000, transcendentals=200_000),
    )(block_input, qkv_weight, grad_attn)


def solution(mesh):
    placed = (P("dp", None), P(None, None, "mp"), P("dp", "mp"))
    return jax.shard_map(
        on_device,
        mesh=mesh,
        in_specs=placed,
        out_specs=(P("dp", None), P(None, "dp", "mp")),
        check_vma=False,
    )
```

time: 80.8 us -> 78.4 us (0.970)
  Pallas kernels: 76.9 us -> 74.2 us
    pallas_call x1, Pallas kernels: 76.9 us -> 74.2 us  [on_device(): pl.pallas_call(kernel, out_shape=(pltpu.VMEM((ROWS, D), BF16), pltpu.VMEM...]
where the time goes in v3:
time: 78.4 us; the launch traced here: 77.4 us
  Pallas kernels  74.2 us (95%)
  local copies, waits for them, and re-layouts  2.48 us (3%)
    pallas_call x1, Pallas kernels, on_device(): pl.pallas_call(kernel, out_shape=(pltpu.VMEM((ROWS, D), BF16), pltpu.VMEM...  74.2 us
    unnamed x2, local copies, waits for them, and re-layouts  2.48 us

profile of v3, /device:TPU:14, one launch (start us, length us, event | category | flops | bytes accessed | tf_op | source)
XLA Modules:
  0.0 77.4 jit_solution(17122754303416541113)
XLA Ops:
  0.6 74.2 %shard_map.50 = (bf16[256,6144]{1,0:T(8,128)(2,1)S(1)}, bf16[3,384,256]{2,1,0:T(8,128)(2,1)S(1)}) custom-call(bf16[256,6144]{1,0:T(8,128)(2,1)} %x_hbm.1, bf16[3,6144,256]{2,1,0:T(8,128)(2,1)} %w_hbm.1, bf16[256,256]{1,0:T(8,128)(2,1)} %g_hbm.1), custom_call_target="tpu_custom_call" | custom-call | flops 7500000256 | bytes 20000000 | tf_op jit(solution)/shard_map/pallas_call | solution.py:394
  74.9 1.7 %copy.7 = bf16[256,6144]{1,0:T(8,128)(2,1)} copy(bf16[256,6144]{1,0:T(8,128)(2,1)S(1)} %get-tuple-element.2) | data formatting | bytes 6291456
  76.6 0.8 %copy.8 = bf16[3,384,256]{2,1,0:T(8,128)(2,1)} copy(bf16[3,384,256]{2,1,0:T(8,128)(2,1)S(1)} %get-tuple-element.3) | data formatting | bytes 1179648

commit v4 on v3

--- a/solution.py
+++ b/solution.py
@@ -23,7 +23,7 @@
 SLICE = 384
 EH = 384
 XROWS = 64
-RZ = 1280
+RZ = 1408
 RY = HALF - RZ
 AZ = 2048
 AY = HALF - AZ
@@ -142,6 +142,11 @@
 
     lax.fori_loop(0, ROWS // XROWS, normed_rows, 0)
 
+    pl.semaphore_wait(barrier, len(neighbours))
+    for i in range(8):
+        cols = pl.ds(pl.multiple_of((i * 2 + 1 - c) * SLICE, 128), SLICE)
+        remote(nv.at[:, cols], nr.at[:, pl.ds(i * SLICE, SLICE)], 2, core_sem.at[0], to_core)
+
     def project(i, carry):
         w_copy(i).wait()
         pv[:, pl.ds(pl.multiple_of(i * INNER, INNER), INNER)] = dot(nv[...], wv[i], 1, 0).astype(BF16)
@@ -154,7 +159,7 @@
         grads = head_grads(pv[:, cols[0]], pv[:, cols[1]], pv[:, cols[2]], gv[:, pl.ds(h * HD, HD)])
         for col, grad in zip(cols, grads):
             gp[:, col] = grad.astype(BF16)
-    pl.semaphore_wait(barrier, len(neighbours))
+    remote(gp, gp2, 2, core_sem.at[1], to_core)
 
     def block_rows(delta, h):
         return pl.ds(pl.multiple_of((z + delta) % NZ * 2 * OWN + h * OWN, OWN), OWN)
@@ -251,17 +256,12 @@
                 tv.at[block_rows(delta, 1 - yh), pl.ds(RZ, 2 * RY)], yx.at[delta], 0, yx_sem.at[delta], to_yh
             )
 
+    terms(RZ, 2 * RY)
+    y_exchange()
     terms(0, RZ)
     z_start(0)
     terms(D - RZ, RZ)
     z_start(1)
-    terms(RZ, RY)
-    terms(HALF, RY)
-    y_exchange()
-    for i in range(8):
-        cols = pl.ds(pl.multiple_of((i * 2 + 1 - c) * SLICE, 128), SLICE)
-        remote(nv.at[:, cols], nr.at[:, pl.ds(i * SLICE, SLICE)], 2, core_sem.at[0], to_core)
-    remote(gp, gp2, 2, core_sem.at[1], to_core)
 
     def b_units(j):
         ys_ = 1 - yl if j == 0 else yl
@@ -297,21 +297,21 @@
         total = bp[j, 0, ch].astype(F32) + rb[j, 1, 1 - ch].astype(F32)
         return total + rb[j, 2, ch].astype(F32)
 
-    own_rows = block_rows(0, yh)
-    hat, inv = normalize(xv[own_rows, :].astype(F32))
-    xh[...] = hat
-    xinv[...] = jnp.broadcast_to(inv, xinv.shape)
     wait_all(nr, core_sem.at[0])
     wait_all(gp2, core_sem.at[1])
     b_units(0)
     b_start(0)
     z_take(0)
+    own_rows = block_rows(0, yh)
+    hat, inv = normalize(xv[own_rows, :].astype(F32))
+    xh[...] = hat
+    xinv[...] = jnp.broadcast_to(inv, xinv.shape)
     y_start()
     b_units(1)
     z_take(1)
-    y_take(0)
     b_take(0)
     b_start(1)
+    y_take(0)
     z_take(2)
     y_take(1)
     for chain in CHAINS:

time: 78.4 us -> 75.9 us (0.968)
  Pallas kernels: 74.2 us -> 71.9 us
    pallas_call x1, Pallas kernels: 74.2 us -> 71.9 us  [on_device(): pl.pallas_call(kernel, out_shape=(pltpu.VMEM((ROWS, D), BF16), pltpu.VMEM...]
where the time goes in v4:
time: 75.9 us; the launch traced here: 75 us
  Pallas kernels  71.9 us (95%)
  local copies, waits for them, and re-layouts  2.48 us (3%)
    pallas_call x1, Pallas kernels, on_device(): pl.pallas_call(kernel, out_shape=(pltpu.VMEM((ROWS, D), BF16), pltpu.VMEM...  71.9 us
    unnamed x2, local copies, waits for them, and re-layouts  2.48 us

profile of v4, /device:TPU:14, one launch (start us, length us, event | category | flops | bytes accessed | tf_op | source)
XLA Modules:
  0.0 75.0 jit_solution(5827350106113412987)
XLA Ops:
  0.6 71.9 %shard_map.50 = (bf16[256,6144]{1,0:T(8,128)(2,1)S(1)}, bf16[3,384,256]{2,1,0:T(8,128)(2,1)S(1)}) custom-call(bf16[256,6144]{1,0:T(8,128)(2,1)} %x_hbm.1, bf16[3,6144,256]{2,1,0:T(8,128)(2,1)} %w_hbm.1, bf16[256,256]{1,0:T(8,128)(2,1)} %g_hbm.1), custom_call_target="tpu_custom_call" | custom-call | flops 7500000256 | bytes 20000000 | tf_op jit(solution)/shard_map/pallas_call | solution.py:394
  72.6 1.7 %copy.7 = bf16[256,6144]{1,0:T(8,128)(2,1)} copy(bf16[256,6144]{1,0:T(8,128)(2,1)S(1)} %get-tuple-element.2) | data formatting | bytes 6291456
  74.2 0.8 %copy.8 = bf16[3,384,256]{2,1,0:T(8,128)(2,1)} copy(bf16[3,384,256]{2,1,0:T(8,128)(2,1)S(1)} %get-tuple-element.3) | data formatting | bytes 1179648
